TPU v7x, 32 devices: a whole 2x2x4 slice. The times are simulated.
32 devices in a mesh: groups: 2 (over y), seq: 4 (over z), chan: 2 (over x), dp: 2 (over core).
Axes of the slice: x: 2, y: 2, z: 4, core: 2. Of those that a mesh axis runs over, the one named last changes fastest.
Arguments:
- conv_input: bfloat16 [4, 2048, 2048], P(('groups', 'dp'), 'seq', 'chan'), parts along dimension 0, may hold values from -6 to 6
- conv_weight: float32 [4, 2048], P(None, 'chan'), may hold values from -3 to 3
- log_decay: float32 [4, 2048, 32], P(('groups', 'dp'), 'seq', 'chan'), parts along dimension 0, as said below
- state_in: bfloat16 [4, 2048, 128], P(('groups', 'dp'), 'seq'), parts along dimension 0, may hold values from -1.5 to 1.5
- state_out: bfloat16 [4, 2048, 128], P(('groups', 'dp'), 'seq'), parts along dimension 0, may hold values from -1.5 to 1.5
- out_grad: bfloat16 [4, 2048, 2048], P(('groups', 'dp'), 'seq', 'chan'), parts along dimension 0, may hold values from -3 to 3
- lengths: int32 [4], P(('groups', 'dp')), parts along dimension 0, may hold values from 1 to 2048, as said below
- segment_starts: int32 [4, 2], P(('groups', 'dp')), parts along dimension 0, may hold values from 1 to 2047
Outputs:
- input_grad: bfloat16 [4, 2048, 2048], P(('groups', 'dp'), 'seq', 'chan'), parts along dimension 0
- state_in_grad: float32 [4, 2048, 128], P(('groups', 'dp'), 'seq'), parts along dimension 0
- state_out_grad: float32 [4, 2048, 128], P(('groups', 'dp'), 'seq'), parts along dimension 0
- weight_grad: float32 [8, 2048], P('groups', 'chan'), parts along dimension 0
There are 2 independent parts, one for each index of `groups`. A program takes and returns all parts, laid end to end along the dimension named above; an argument that names none is the same for every part. Nothing has to cross between parts.
Inputs may be any that keep to these rules, and one draw needn't show every extreme that they name: `lengths`: at least one series of a group runs the full 2048 steps. `log_decay`: strictly negative.
All inputs are finite; a program needn't handle non-finite values.
Results may differ from a plain program's by a relative error of at most 0.019.
Values may be sent and summed in bfloat16 or wider, within the bound.
A program may use at most 128 MiB of HBM per device.

v0:
```python
import math

import jax
import jax.numpy as jnp
from jax import lax
from jax.sharding import PartitionSpec as P

BLOCK = 256


def shifted(block, axis, distance):
    devices = range(lax.axis_size(axis))
    route = [(i - distance, i) for i in devices if i - distance in devices]
    return lax.ppermute(block, axis, route)


def prefix(part, axis, combine, identity, reverse):
    count = lax.axis_size(axis)
    place = lax.axis_index(axis)
    ahead = count - 1 - place if reverse else place
    gathered = jax.tree.map(lambda a: lax.all_gather(a, axis), part)
    state = jax.tree.map(lambda a, e: jnp.zeros_like(a) + jnp.asarray(e, a.dtype), part, identity)

    def one(hop, state):
        source = count - 1 - hop if reverse else hop
        return combine(
            state, jax.tree.map(lambda a: lax.dynamic_index_in_dim(a, source, 0, False), gathered)
        )

    return lax.fori_loop(0, ahead, one, state)


def block_decay(logs, resets):
    kept = jnp.where(resets[:, :, None], jnp.float32(0.0), logs)
    running = jnp.cumsum(kept, axis=1)
    segment = jnp.cumsum(resets.astype(jnp.int32), axis=1)
    steps = logs.shape[1]
    order = jnp.arange(steps, dtype=jnp.int32)
    final = running[:, -1:, :]
    final_seg = segment[:, -1:]
    start_decay = jnp.where((segment == 0)[:, :, None], jnp.exp(running), jnp.float32(0.0))
    end_decay = jnp.where(
        (segment == final_seg)[:, :, None], jnp.exp(final - running), jnp.float32(0.0)
    )
    whole = jnp.where(final_seg == 0, jnp.exp(final[:, 0, :]), jnp.float32(0.0))
    per_head = jnp.transpose(running, (0, 2, 1))
    spread = per_head[:, :, :, None] - per_head[:, :, None, :]
    linked = (segment[:, :, None] == segment[:, None, :]) & (order[:, None] >= order[None, :])[None]
    linked = linked[:, None]
    decay_map = jnp.where(
        linked, jnp.exp(jnp.where(linked, spread, jnp.float32(0.0))), jnp.float32(0.0)
    )
    return (decay_map, start_decay, end_decay, whole)


def split_pair(values):
    upper = values.astype(jnp.bfloat16)
    lower = (values - upper.astype(jnp.float32)).astype(jnp.bfloat16)
    return (upper, lower)


def pair_product(form, left, right):
    upper, lower = left
    return jnp.einsum(form, upper, right, preferred_element_type=jnp.float32) + jnp.einsum(
        form, lower, right, preferred_element_type=jnp.float32
    )


def block_state(values, matrix, decay):
    scaled = decay[..., None] * values.astype(jnp.float32)
    return pair_product("bshp,bsn->bhpn", split_pair(scaled), matrix)


def compose(earlier, later):
    return (earlier[0] * later[0], later[0][:, :, None, None] * earlier[1] + later[1])


def block_outputs(
    scan_in, masked, in_mat, out_mat, decay_map, start_decay, end_decay, state, grad_state
):
    scores = jnp.einsum("bthp,bshp->bhts", masked, scan_in, preferred_element_type=jnp.float32)
    weighted = (scores * decay_map).astype(jnp.bfloat16)
    inner = jnp.einsum("btn,bsn->bts", out_mat, in_mat, preferred_element_type=jnp.float32)
    carried = (inner[:, None] * decay_map).astype(jnp.bfloat16)
    scaled_grads = start_decay[..., None] * masked.astype(jnp.float32)
    scaled_scan = end_decay[..., None] * scan_in.astype(jnp.float32)
    state_pair = split_pair(state)
    grad_pair = split_pair(grad_state)
    out_part = jnp.einsum("bhts,bsn->btn", weighted, in_mat, preferred_element_type=jnp.float32)
    out_part = out_part + pair_product("bthp,bhpn->btn", split_pair(scaled_grads), state_pair[0])
    out_part = out_part + pair_product("bthp,bhpn->btn", split_pair(scaled_grads), state_pair[1])
    in_part = jnp.einsum("bhrt,brn->btn", weighted, out_mat, preferred_element_type=jnp.float32)
    in_part = in_part + pair_product("bthp,bhpn->btn", split_pair(scaled_scan), grad_pair[0])
    in_part = in_part + pair_product("bthp,bhpn->btn", split_pair(scaled_scan), grad_pair[1])
    scan_grad = jnp.einsum("bhrt,brhp->bthp", carried, masked, preferred_element_type=jnp.float32)
    scan_grad = scan_grad + end_decay[..., None] * pair_product("bhpn,btn->bthp", grad_pair, in_mat)
    return (out_part, in_part, scan_grad)


def backward_conv(padded, weights, count):
    kernel = weights.shape[0]
    summed = jnp.zeros((padded.shape[0], count, padded.shape[2]), jnp.float32)
    for offset in range(kernel):
        start = kernel - 1 - offset
        summed = summed + weights[offset] * padded[:, start : start + count].astype(jnp.float32)
    return summed.astype(jnp.bfloat16)


def per_device(
    conv_input, conv_weight, log_decay, state_in, state_out, out_grad, lengths, segment_starts
):
    batch, local, channels = conv_input.shape
    heads = log_decay.shape[2]
    width = channels // heads
    states = state_in.shape[2]
    kernel = conv_weight.shape[0]
    seq_count = lax.axis_size("seq")
    seq_index = lax.axis_index("seq")
    rim = shifted(conv_input[:, local - (kernel - 1) :, :], "seq", 1)
    padded = jnp.concatenate([rim, conv_input], axis=1)
    mixed = jnp.zeros((batch, local, channels), jnp.float32)
    for offset in range(kernel):
        mixed = mixed + conv_weight[offset] * padded[:, offset : offset + local].astype(jnp.float32)
    position = seq_index * local + jnp.arange(local, dtype=jnp.int32)
    valid = (position[None, :] < lengths[:, None])[:, :, None]
    resets = jnp.any(segment_starts[:, None, :] == position[None, :, None], axis=2)
    gain = jnp.where(resets[:, :, None], jnp.float32(1.0), jnp.sqrt(-jnp.expm1(2.0 * log_decay)))
    sigmoid_u = jax.nn.sigmoid(mixed)
    activated = ((mixed * sigmoid_u).reshape(batch, local, heads, width) * gain[..., None]).reshape(
        batch, local, channels
    )
    scan_in = (
        jnp.where(valid, activated, jnp.float32(0.0))
        .astype(jnp.bfloat16)
        .reshape(batch, local, heads, width)
    )
    masked = jnp.where(valid, out_grad, jnp.zeros_like(out_grad)).reshape(
        batch, local, heads, width
    )
    count = local // BLOCK
    records = []
    carried_decay = jnp.ones((batch, heads), jnp.float32)
    forward_sum = jnp.zeros((batch, heads, width, states), jnp.float32)
    backward_sum = jnp.zeros((batch, heads, width, states), jnp.float32)
    for index in range(count):
        span = slice(index * BLOCK, (index + 1) * BLOCK)
        decay_map, start_decay, end_decay, whole = block_decay(log_decay[:, span], resets[:, span])
        pushed = block_state(scan_in[:, span], state_in[:, span], end_decay)
        pulled = block_state(masked[:, span], state_out[:, span], start_decay)
        records.append((span, decay_map, start_decay, end_decay, whole, pushed, pulled))
        forward_sum = whole[:, :, None, None] * forward_sum + pushed
        carried_decay = carried_decay * whole
    for record in reversed(records):
        backward_sum = record[4][:, :, None, None] * backward_sum + record[6]
    identity = (jnp.ones_like(carried_decay), jnp.zeros_like(forward_sum))
    _, entering = prefix((carried_decay, forward_sum), "seq", compose, identity, False)
    _, leaving = prefix((carried_decay, backward_sum), "seq", compose, identity, True)
    state_now = entering
    entries = []
    for record in records:
        entries.append(state_now)
        state_now = record[4][:, :, None, None] * state_now + record[5]
    grad_now = leaving
    exits = [grad_now] * count
    for index in reversed(range(count)):
        exits[index] = grad_now
        grad_now = records[index][4][:, :, None, None] * grad_now + records[index][6]
    out_list = []
    in_list = []
    scan_list = []
    for index in range(count):
        span, decay_map, start_decay, end_decay, whole, pushed, pulled = records[index]
        out_part, in_part, scan_grad = block_outputs(
            scan_in[:, span],
            masked[:, span],
            state_in[:, span],
            state_out[:, span],
            decay_map,
            start_decay,
            end_decay,
            entries[index],
            exits[index],
        )
        out_list.append(out_part)
        in_list.append(in_part)
        scan_list.append(scan_grad)
    out_local = jnp.concatenate(out_list, axis=1)
    in_local = jnp.concatenate(in_list, axis=1)
    scan_grad = jnp.concatenate(scan_list, axis=1)
    state_in_grad, state_out_grad = (
        lax.psum(in_local.astype(jnp.bfloat16), "chan").astype(jnp.float32),
        lax.psum(out_local.astype(jnp.bfloat16), "chan").astype(jnp.float32),
    )
    slope = sigmoid_u * (1.0 + mixed * (1.0 - sigmoid_u))
    mixed_grad = (scan_grad * gain[..., None]).reshape(batch, local, channels) * slope
    mixed_grad = jnp.where(valid, mixed_grad, jnp.float32(0.0)).astype(jnp.bfloat16)
    after = shifted(mixed_grad[:, : kernel - 1, :], "seq", -1)
    input_grad = backward_conv(jnp.concatenate([mixed_grad, after], axis=1), conv_weight, local)
    wide_grad = mixed_grad.astype(jnp.float32)
    rows = []
    for offset in range(kernel):
        rows.append(
            jnp.sum(wide_grad * padded[:, offset : offset + local].astype(jnp.float32), axis=(0, 1))
        )
    factor = 1.0 / math.sqrt(batch * lax.axis_size("dp") * local * seq_count)
    weight_grad = lax.psum(jnp.stack(rows) * factor, ("seq", "dp"))
    return (input_grad, state_in_grad, state_out_grad, weight_grad)


def solution(mesh):
    placed = (
        P(("groups", "dp"), "seq", "chan"),
        P(None, "chan"),
        P(("groups", "dp"), "seq", "chan"),
        P(("groups", "dp"), "seq", None),
        P(("groups", "dp"), "seq", None),
        P(("groups", "dp"), "seq", "chan"),
        P(("groups", "dp")),
        P(("groups", "dp"), None),
    )
    return jax.shard_map(
        per_device,
        mesh=mesh,
        in_specs=placed,
        out_specs=(
            P(("groups", "dp"), "seq", "chan"),
            P(("groups", "dp"), "seq", None),
            P(("groups", "dp"), "seq", None),
            P("groups", "chan"),
        ),
        check_vma=False,
    )
```

profile of v0, /device:TPU:0, one launch (start us, length us, event | category | flops | bytes accessed | tf_op | source)
XLA Modules:
  0.0 183.1 jit_solution(17551655215464907712)
XLA Ops:
  7.2 0.7 compare_reduce_fusion
  8.0 0.7 slice_select_fusion
  18.6 1.5 copy.104
  22.4 1.1 fusion.37
  23.7 0.8 slice.146
  24.4 0.9 copy.122
  25.3 5.6 %collective-permute-start = (bf16[1,3,1024]{1,2,0:T(8,128)(2,1)}, bf16[1,3,1024]{1,2,0:T(8,128)(2,1)}, u32[]{:S(2)}, u32[]{:S(2)}) collective-permute-start(bf16[1,3,1024]{1,2,0:T(8,128)(2,1)} %copy.122), channel_id=1, source_target_pairs={{0,4},{4,8},{8,12},{1,5},{5,9},{9,13},{2,6},{6,10},{10,14},{3,7},{... | collective-permute-start | bytes 18440 | tf_op jit(solution)/shard_map/ppermute | solution.py:14
  31.0 1.5 copy.123
  32.9 13.7 %all_gather.18 = f32[4,1,16]{2,1,0:T(1,128)} all-gather(f32[1,1,16]{2,1,0:T(1,128)S(1)} %mul.350), channel_id=1, replica_groups=mesh['groups'=2,'seq'=4,'chan'=2,'dp'=2] {'seq'}, dimensions={0}, use_global_device_ids=true | all-gather | bytes 320 | tf_op jit(solution)/shard_map/all_gather | solution.py:21
  49.3 0.9 fusion.158
  50.2 0.9 fusion.145
  51.1 21.5 %all-gather.5.cloned.1.call-done = f32[64,64,128]{2,1,0:T(8,128)} async-done(((f32[16,64,128]{2,1,0:T(8,128)}), f32[64,64,128]{2,1,0:T(8,128)}) %all-gather.5.cloned.1.call-update) | async-done | bytes 2097168 | tf_op jit(solution)/shard_map/all_gather | solution.py:21
  72.6 5.5 %while.26 = (s32[]{:T(128)}, f32[1,16,64,128]{3,2,1,0:T(8,128)S(1)}, s32[]{:T(128)}, f32[4,1,16]{2,1,0:T(1,128)}, f32[4,1,16,64,128]{4,3,2,1,0:T(8,128)}, /*index=5*/s32[]{:T(128)}, s32[]{:T(128)}, s32[]{:T(128)}, s32[]{:T(128)}) while((s32[]{:T(128)}, f32[1,16,64,128]{3,2,1,0:T(8,128)S(1)}, s32[]{:T(128)}, f32[4,1,16]{2,1,0:T(1,128)}, ...), condition=%wide.region_10.11_spmd, body=%wide.region_9.10_spmd.sunk | while | flops 262150 | bytes 1573203 | solution.py:30
  73.2 1.2 bitcast_add_fusion.12
  75.0 1.2 bitcast_add_fusion.12
  76.9 1.2 bitcast_add_fusion.12
  79.8 1.3 fusion.34
  81.2 1.3 fusion.35
  82.6 6.2 %fusion.12 = (f32[1024]{0:T(1024)S(1)}, f32[1024]{0:T(1024)S(1)}, f32[1024]{0:T(1024)S(1)}, f32[1024]{0:T(1024)S(1)}, bf16[1,512,1024]{1,2,0:T(8,128)(2,1)}, /*index=5*/f32[1,512,1024]{1,2,0:T(8,128)S(1)}) fusion(bf16[1,512,1024]{1,2,0:T(8,128)(2,1)S(1)} %copy.123, bf16[1,3,1024]{1,2,0:T(8,128)(2,1)} %collective-permute-done, ...), kind=kLoop, calls=%fused_computation.35 | loop fusion | flops 25686016 | bytes 6363648 | tf_op jit(solution)/shard_map/reduce_sum | solution.py:203
  90.5 1.1 fusion.36
  91.7 1.7 slice.175
  93.3 1.3 collective-permute-start.1
  94.7 40.0 %psum.23 = f32[4,1024]{1,0:T(4,128)} all-reduce(f32[4,1024]{1,0:T(4,128)S(1)} %maximum_multiply_fusion), channel_id=1, replica_groups=mesh['groups'=2,'seq'=4,'chan'=2,'dp'=2] {'seq','dp'}, use_global_device_ids=true, to_apply=%region_21.22 | all-reduce | flops 4096 | bytes 32768 | tf_op jit(solution)/shard_map/psum | solution.py:206
  134.6 1.4 convolution_bitcast_fusion.14
  136.1 1.6 convolution_bitcast_fusion.12
  138.4 1.6 convert_reduce_fusion.1
  141.7 1.6 convert_reduce_fusion
  149.2 3.9 %fusion.11 = bf16[1,512,1024]{1,2,0:T(8,128)(2,1)S(1)} fusion(bf16[1,512,1024]{1,2,0:T(8,128)(2,1)S(1)} %copy-done, bf16[1,3,1024]{1,2,0:T(8,128)(2,1)} %collective-permute-done.1, f32[1024]{0:T(1024)S(1)} %bitcast.442, f32[1024]{0:T(1024)S(1)} %bitcast.444, f32[1024]{0:T(1024)S(1)} %bitcast.440, f32[1024]{0:T(1024)S(1)} %bitcast.438), kind=kLoop, calls=%fused_computation.34 | loop fusion | flops 11010048 | bytes 2119680 | tf_op jit(solution)/shard_map/convert_element_type | solution.py:106
  153.1 1.3 copy.126
  154.4 19.0 %all-reduce.3.cloned.1.call-done = (bf16[1,512,128]{2,1,0:T(8,128)(2,1)}, bf16[1,512,128]{2,1,0:T(8,128)(2,1)}) async-done(((bf16[1,512,128]{2,1,0:T(8,128)(2,1)}, bf16[1,512,128]{2,1,0:T(8,128)(2,1)}), (bf16[1,512,128]{2,1,0:T(8,128)(2,1)}, bf16[1,512,128]{2,1,0:T(8,128)(2,1)})) %all-reduce.3.cloned.1.call-update) | async-done | bytes 262160 | tf_op jit(solution)/shard_map/psum | solution.py:191
  173.3 1.6 convert_element_type.247
  175.0 1.6 convert_element_type.254
  (200 shorter events, 25.0 us)
Async XLA Ops:
  7.2 65.4 %all-gather.5.cloned.1.call-start = ((), (), s32[]{:S(2)}) async-start(), calls=%async_computation | async-start | bytes 2621440 | tf_op jit(solution)/shard_map/all_gather | solution.py:21
  13.6 4.9 %copy-start.31 = (s32[256]{0:T(256)}, s32[256]{0:T(256)S(1)}, u32[]{:S(2)}) copy-start(s32[256]{0:T(256)S(1)} %get-tuple-element.233) | copy-start | bytes 3076
  17.9 2.7 %copy-start.9 = (f32[1,256,16]{1,2,0:T(8,128)}, f32[1,256,16]{1,2,0:T(8,128)S(1)}, u32[]{:S(2)}) copy-start(f32[1,256,16]{1,2,0:T(8,128)S(1)} %copy.155) | copy-start | bytes 49156
  18.6 1.6 copy-start.41
  18.6 1.6 copy-start.4
  21.0 1.4 copy-start.11
  23.6 23.0 %copy-start.30 = (f32[4,1024]{1,0:T(4,128)S(1)}, f32[4,1024]{1,0:T(4,128)}, u32[]{:S(2)}) copy-start(f32[4,1024]{1,0:T(4,128)} %param.13) | copy-start | bytes 49156
  23.6 24.8 %copy-start.13 = (f32[1,512,16]{1,2,0:T(8,128)S(1)}, f32[1,512,16]{1,2,0:T(8,128)}, u32[]{:S(2)}) copy-start(f32[1,512,16]{1,2,0:T(8,128)} %param.14) | copy-start | bytes 98308
  23.6 24.8 %copy-start.36 = (pred[512]{0:T(512)(128)(4,1)S(1)}, pred[512]{0:T(512)(128)(4,1)}, u32[]{:S(2)}) copy-start(pred[512]{0:T(512)(128)(4,1)} %copy-done.35) | copy-start | bytes 1540
  23.6 24.8 %copy-start.32 = (s32[256]{0:T(256)S(1)}, s32[256]{0:T(256)}, u32[]{:S(2)}) copy-start(s32[256]{0:T(256)} %copy-done.31) | copy-start | bytes 3076
  23.6 25.6 %copy-start.34 = (s32[256]{0:T(256)S(1)}, s32[256]{0:T(256)}, u32[]{:S(2)}) copy-start(s32[256]{0:T(256)} %copy-done.33) | copy-start | bytes 3076
  23.6 25.7 %copy-start.3 = (bf16[1,512,128]{2,1,0:T(8,128)(2,1)S(1)}, bf16[1,512,128]{2,1,0:T(8,128)(2,1)}, u32[]{:S(2)}) copy-start(bf16[1,512,128]{2,1,0:T(8,128)(2,1)} %param.15) | copy-start | bytes 393220
  23.6 120.6 %all-gather.7.cloned.1.call-start = ((), (), s32[]{:S(2)}) async-start(), calls=%async_computation.1 | async-start | bytes 2621440 | tf_op jit(solution)/shard_map/all_gather | solution.py:21
  25.3 57.2 %collective-permute-start = (bf16[1,3,1024]{1,2,0:T(8,128)(2,1)}, bf16[1,3,1024]{1,2,0:T(8,128)(2,1)}, u32[]{:S(2)}, u32[]{:S(2)}) collective-permute-start(bf16[1,3,1024]{1,2,0:T(8,128)(2,1)} %copy.122), channel_id=1, source_target_pairs={{0,4},{4,8},{8,12},{1,5},{5,9},{9,13},{2,6},{6,10},{10,14},{3,7},{... | collective-permute-start | bytes 18440 | tf_op jit(solution)/shard_map/ppermute | solution.py:14
  49.3 31.9 %copy-start.14 = (pred[256,256]{1,0:T(8,128)(4,1)}, pred[256,256]{1,0:T(8,128)(4,1)S(1)}, u32[]{:S(2)}) copy-start(pred[256,256]{1,0:T(8,128)(4,1)S(1)} %fusion.110) | copy-start | bytes 196612
  72.6 5.8 %copy-start.39 = (f32[16]{0:T(128)S(1)}, f32[16]{0:T(128)}, u32[]{:S(2)}) copy-start(f32[16]{0:T(128)} %get-tuple-element.255) | copy-start | bytes 196
  81.2 1.4 copy-start.18
  81.2 1.4 copy-start.20
  81.2 1.4 copy-start.22
  81.2 1.4 copy-start.24
  81.2 1.4 copy-start.42
  91.6 81.7 %all-reduce.3.cloned.1.call-start = ((), (), s32[]{:S(2)}) async-start(), calls=%async_computation.2 | async-start | bytes 524288 | tf_op jit(solution)/shard_map/psum | solution.py:191
  93.3 55.8 %collective-permute-start.1 = (bf16[1,3,1024]{1,2,0:T(8,128)(2,1)}, bf16[1,3,1024]{1,2,0:T(8,128)(2,1)}, u32[]{:S(2)}, u32[]{:S(2)}) collective-permute-start(bf16[1,3,1024]{1,2,0:T(8,128)(2,1)} %slice.175), channel_id=1, source_target_pairs={{4,0},{8,4},{12,8},{5,1},{9,5},{13,9},{6,2},{10,6},{14,10},{7,3},{... | collective-permute-start | bytes 18440 | tf_op jit(solution)/shard_map/ppermute | solution.py:14
  134.6 3.1 %copy-start.2 = (f32[1,16,64,128]{3,2,1,0:T(8,128)S(1)}, f32[1,16,64,128]{3,2,1,0:T(8,128)}, u32[]{:S(2)}) copy-start(f32[1,16,64,128]{3,2,1,0:T(8,128)} %copy-done.1) | copy-start | bytes 1572868
  136.1 2.3 %copy-start.17 = (pred[256,256]{1,0:T(8,128)(4,1)S(1)}, pred[256,256]{1,0:T(8,128)(4,1)}, u32[]{:S(2)}) copy-start(pred[256,256]{1,0:T(8,128)(4,1)} %fusion.111) | copy-start | bytes 196612
  136.1 2.3 %copy-start.29 = (f32[16,256]{1,0:T(8,128)S(1)}, f32[16,256]{1,0:T(8,128)}, u32[]{:S(2)}) copy-start(f32[16,256]{1,0:T(8,128)} %bitcast_add_fusion.5) | copy-start | bytes 49156
  144.4 1.4 copy-start.38
  147.3 1.8 copy-start
  147.3 1.8 copy-start.19
  147.3 1.8 copy-start.21
  147.3 1.8 copy-start.23
  147.3 1.8 copy-start.25
  (17 other events, 16.6 us)
Sparse Core Ops, SparseCore 0:
  23.7 48.7 all-gather.4
  91.7 46.4 all-gather.6
  149.2 24.0 all-reduce.2
where the time goes:
time: 184 us; the launch traced here: 183 us
  blocking collectives  53.6 us (29%)
  waiting for transfers between devices  40.5 us (22%)
  other arithmetic  26.6 us (14%)
  matrix products  21.6 us (12%)
  between operations  18 us (10%)
  local copies, waits for them, and re-layouts  15.7 us (9%)
  starting transfers between devices  7.02 us (4%)
    psum x1, blocking collectives, per_device(): weight_grad = lax.psum(jnp.stack(rows) * factor, ('seq', 'dp'))  40 us
    all_gather x2, waiting for transfers between devices, prefix(): gathered = jax.tree.map(lambda a: lax.all_gather(a, axis), part)  21.5 us
    psum x1, waiting for transfers between devices, per_device(): lax.psum(in_local.astype(jnp.bfloat16), 'chan').astype(jnp.float32)  19 us
    all_gather x1, blocking collectives, prefix(): gathered = jax.tree.map(lambda a: lax.all_gather(a, axis), part)  13.7 us
    dot_general x14, matrix products, pair_product(): jnp.einsum(form, lower, right, preferred_element_type=jnp.float32)  8.56 us
    ppermute x2, starting transfers between devices, shifted(): return lax.ppermute(block, axis, route)  6.9 us
    reduce_sum x1, other arithmetic, per_device(): jnp.sum(wide_grad * padded[:, offset:offset + local].astype(jnp.float32),...  6.22 us
    unnamed x95, local copies, waits for them, and re-layouts  6.05 us
  transfers between devices with their start and end apart: 5, of which 2 were waited for; matrix products, arithmetic and copies ran while one was open for 21% of the time, Pallas kernels for 0%

commit v1 on v0

v1 whole, which is shorter than its diff:
```python
import functools
import math

import jax
import jax.numpy as jnp
from jax import lax
from jax.experimental import pallas as pl
from jax.experimental.pallas import tpu as pltpu
from jax.sharding import PartitionSpec as P

BLOCK = 256
GROUP = 256
F32 = jnp.float32
BF16 = jnp.bfloat16
MESH = pl.DeviceIdType.MESH
LANES = (((1,), (1,)), ((), ()))


def dot(a, b):
    return jnp.dot(a, b, preferred_element_type=F32)


def dot_lanes(a, b):
    return lax.dot_general(a, b, LANES, preferred_element_type=F32)


def iota(shape, dim):
    return lax.broadcasted_iota(jnp.int32, shape, dim)


def pack(values):
    upper = values.astype(BF16)
    lower = (values - upper.astype(F32)).astype(BF16)
    return jnp.concatenate([upper, lower], axis=1)


def one_minus_exp(y):
    series = 1.0 / 5040.0
    for term in (720.0, 120.0, 24.0, 6.0, 2.0, 1.0):
        series = series * y + 1.0 / term
    return jnp.where(y > -0.35, -y * series, 1.0 - jnp.exp(y))


def kernel(
    seq_n, chan_n, dp_n,
    x_ref, w_ref, ld_ref, bi_ref, co_ref, og_ref, len_ref, st_ref,
    ig_ref, sig_ref, sog_ref, wg_ref,
    rim_in, xpad, mgpad, gs, ee, sgrad, colb, rowb, mask, inner, wsum,
    packs, whole, scan, sg, ss, push, pull, lead,
    f_out, f_in, b_out, b_in, cbuf, mg_out, mg_in, wbuf,
    x_sem, f_sem, b_sem, m_sem, c_send, c_recv, w_send, w_recv,
):
    local, channels = x_ref.shape
    heads = ld_ref.shape[1]
    width = channels // heads
    taps = w_ref.shape[0]
    blocks = local // BLOCK
    groups = channels // GROUP
    pairs = channels // 128
    per = 128 // width
    starts = st_ref.shape[1]
    team = seq_n * dp_n
    seq = lax.axis_index("seq")
    chan = lax.axis_index("chan")
    core = lax.axis_index("dp")
    mine = seq * dp_n + core

    def member(step):
        other = lax.rem(mine + step, team)
        return {"seq": lax.div(other, dp_n), "dp": lax.rem(other, dp_n)}

    def peer(step):
        return {"chan": lax.rem(chan + step, chan_n)}

    barrier = pltpu.get_barrier_semaphore()

    def greet(step, carry):
        pl.semaphore_signal(barrier, inc=1, device_id=member(step), device_id_type=MESH)
        return carry

    lax.fori_loop(1, team, greet, 0)
    for step in range(1, chan_n):
        pl.semaphore_signal(barrier, inc=1, device_id=peer(step), device_id_type=MESH)

    def remote(src, dst, send, recv, target):
        return pltpu.make_async_remote_copy(
            src_ref=src, dst_ref=dst, send_sem=send, recv_sem=recv,
            device_id=target, device_id_type=MESH,
        )

    def spans(b):
        return pl.ds(b * BLOCK, BLOCK)

    length = len_ref[0]
    for b in range(blocks):
        base = seq * local + b * BLOCK
        shape = (BLOCK, heads)
        place = base + iota(shape, 0)
        reset = place == st_ref[0, 0]
        for j in range(1, starts):
            reset = reset | (place == st_ref[0, j])

        def segments(pos):
            total = jnp.zeros(pos.shape, jnp.int32)
            for j in range(starts):
                begin = st_ref[0, j]
                total = total + ((pos >= begin) & (base <= begin)).astype(jnp.int32)
            return total

        segment = segments(place)
        logs = ld_ref[spans(b), :]
        kept = jnp.where(reset, 0.0, logs)
        order_r = iota((BLOCK, BLOCK), 0)
        order_c = iota((BLOCK, BLOCK), 1)
        tri = (order_r >= order_c).astype(F32)
        running = lax.dot_general(
            tri, kept, (((1,), (0,)), ((), ())),
            precision=lax.Precision.HIGHEST, preferred_element_type=F32,
        )
        final = running[BLOCK - 1 :, :]
        start = jnp.where(segment == 0, jnp.exp(running), 0.0)
        end = jnp.where(segment == segment[BLOCK - 1 :, :], jnp.exp(final - running), 0.0)
        valid = place < length
        gain = jnp.where(reset, 1.0, jnp.sqrt(one_minus_exp(2.0 * logs)))
        packs[0, spans(b), :] = pack(jnp.where(valid, start, 0.0))
        packs[1, spans(b), :] = pack(end)
        packs[2, spans(b), :] = pack(jnp.where(valid, gain, 0.0))
        last = jnp.broadcast_to(start[BLOCK - 1 :, :], (16, heads))
        spread_e = (lax.rem(iota((2 * heads, channels), 0), heads)
                    == lax.div(iota((2 * heads, channels), 1), width)).astype(BF16)
        whole[b] = dot(pack(last), spread_e)[:8]
        turned = jnp.transpose(running)
        for h in range(heads):
            colb[h, spans(b), :] = jnp.broadcast_to(running[:, h : h + 1], (BLOCK, 128))
            rowb[b, h] = turned[h : h + 1, :]
        pos_s = base + order_r
        pos_t = base + order_c
        linked = (order_c >= order_r) & (segments(pos_s) == segments(pos_t)) & (pos_t < length)
        mask[b] = jnp.where(linked, 0.0, -jnp.inf)
        inner[b] = dot_lanes(bi_ref[spans(b), :], co_ref[spans(b), :])
        wsum[b] = jnp.zeros((BLOCK, BLOCK), F32)

    def lanes(g):
        return pl.ds(pl.multiple_of(g * GROUP, GROUP), GROUP)

    def spread(g):
        shape = (2 * heads, GROUP)
        head = lax.rem(iota(shape, 0), heads)
        return (head == lax.div(iota(shape, 1) + g * GROUP, width)).astype(BF16)

    pl.semaphore_wait(barrier, team - 1 + chan_n - 1)

    tail = pl.ds(local - 16, 16)

    def rim_copy():
        return remote(x_ref.at[tail], rim_in, x_sem.at[0], x_sem.at[1], {"seq": seq + 1})

    @pl.when(seq < seq_n - 1)
    def _():
        rim_copy().start()

    def f_copy(c):
        return remote(f_out.at[c], f_in.at[c], f_sem.at[0, c], f_sem.at[1, c], {"seq": seq + 1})

    def b_copy(c):
        return remote(b_out.at[c], b_in.at[c], b_sem.at[0, c], b_sem.at[1, c], {"seq": seq - 1})

    def advance(c):
        state = f_in[c].astype(F32)
        for b in range(blocks):
            state = whole[b, 0:1, lanes(c)] * state + push[b, c]
        f_out[c] = state.astype(BF16)

    def retreat(c):
        state = b_in[c].astype(F32)
        for b in reversed(range(blocks)):
            state = whole[b, 0:1, lanes(c)] * state + pull[b, c]
        b_out[c] = state.astype(BF16)

    outs_t = [jnp.transpose(co_ref[spans(b), :].astype(F32)).astype(BF16) for b in range(blocks)]

    @pl.when(seq == seq_n - 1)
    def _():
        b_in[...] = jnp.zeros(b_in.shape, BF16)

    def pulled(g, carry):
        e = spread(g)
        for b in range(blocks):
            scaled = (dot(packs[0, spans(b), :], e) * og_ref[spans(b), lanes(g)].astype(F32)).astype(BF16)
            sg[spans(b), lanes(g)] = scaled
            pull[b, g] = dot(outs_t[b], scaled)

        @pl.when((seq == seq_n - 1) & (seq > 0))
        def _():
            retreat(g)
            b_copy(g).start()

        return carry

    lax.fori_loop(0, groups, pulled, 0)

    xpad[pl.ds(8, local), :] = x_ref[...].astype(F32)

    @pl.when(seq == 0)
    def _():
        xpad[pl.ds(0, 8), :] = jnp.zeros((8, channels), F32)
        f_in[...] = jnp.zeros(f_in.shape, BF16)

    @pl.when(seq > 0)
    def _():
        rim_copy().wait_recv()
        xpad[pl.ds(0, 8), :] = rim_in[...].astype(F32)[8:]

    ins_t = [jnp.transpose(bi_ref[spans(b), :].astype(F32)).astype(BF16) for b in range(blocks)]

    def shifted(b, k, g):
        return xpad[pl.ds(8 + b * BLOCK - (taps - 1) + k, BLOCK), lanes(g)]

    def pushed(g, carry):
        e = spread(g)
        for b in range(blocks):
            mixed = w_ref[0:1, lanes(g)] * shifted(b, 0, g)
            for k in range(1, taps):
                mixed = mixed + w_ref[k : k + 1, lanes(g)] * shifted(b, k, g)
            gate = 0.5 + 0.5 * jnp.tanh(0.5 * mixed)
            gain = dot(packs[2, spans(b), :], e)
            end = dot(packs[1, spans(b), :], e)
            act = (mixed * gate * gain).astype(BF16)
            scan[spans(b), lanes(g)] = act
            gs[spans(b), lanes(g)] = gain * gate * (1.0 + mixed * (1.0 - gate))
            ee[spans(b), lanes(g)] = end
            scaled = (end * act.astype(F32)).astype(BF16)
            ss[spans(b), lanes(g)] = scaled
            push[b, g] = dot(ins_t[b], scaled)

        @pl.when((seq == 0) & (seq < seq_n - 1))
        def _():
            advance(g)
            f_copy(g).start()

        return carry

    lax.fori_loop(0, groups, pushed, 0)

    hop = 2
    first = 1

    def work(p):
        pair = pl.ds(pl.multiple_of(p * 128, 128), 128)
        for b in range(blocks):
            scan_p = scan[spans(b), pair]
            grad_p = og_ref[spans(b), pair]
            side = lax.div(iota((BLOCK, 128), 1), width)
            total = jnp.zeros((BLOCK, 128), F32)
            weights = wsum[b]
            for j in range(per):
                h = p * per + j
                scan_h = jnp.where(side == j, scan_p, jnp.zeros_like(scan_p))
                grad_h = jnp.where(side == j, grad_p, jnp.zeros_like(grad_p))
                scores = dot_lanes(scan_h, grad_p)
                column = colb[h, spans(b), :]
                column = jnp.concatenate([column] * (BLOCK // 128), axis=1)
                decay = jnp.exp((rowb[b, h] - column) + mask[b])
                weights = weights + scores * decay
                total = total + dot((inner[b] * decay).astype(BF16), grad_h)
            wsum[b] = weights
            sgrad[spans(b), pair] = total

    def step(k, carry):
        @pl.when(k < pairs)
        def _():
            work(k)

        c_f = k - first - hop * (seq - 1)

        @pl.when((seq > 0) & (c_f >= 0) & (c_f < groups))
        def _():
            f_copy(c_f).wait_recv()

            @pl.when(seq < seq_n - 1)
            def _():
                advance(c_f)
                f_copy(c_f).start()

        c_b = k - hop * (seq_n - 2 - seq)

        @pl.when((seq < seq_n - 1) & (c_b >= 0) & (c_b < groups))
        def _():
            b_copy(c_b).wait_recv()

            @pl.when(seq > 0)
            def _():
                retreat(c_b)
                b_copy(c_b).start()

        return carry

    steps = max(pairs, first + hop * max(seq_n - 2, 0) + groups)
    lax.fori_loop(0, steps, step, 0)

    in_acc = []
    out_acc = []
    for b in range(blocks):
        weights = wsum[b]
        in_acc.append(dot(weights.astype(BF16), co_ref[spans(b), :]))
        out_acc.append(dot(jnp.transpose(weights).astype(BF16), bi_ref[spans(b), :]))
    for c in range(groups):
        part = slice(c * GROUP, (c + 1) * GROUP)
        state = f_in[c]
        for b in range(blocks):
            out_acc[b] = out_acc[b] + dot_lanes(sg[spans(b), part], state)
            if b < blocks - 1:
                state = (whole[b, 0:1, part] * state.astype(F32) + push[b, c]).astype(BF16)
        state = b_in[c]
        for b in reversed(range(blocks)):
            lead[b, c] = state
            in_acc[b] = in_acc[b] + dot_lanes(ss[spans(b), part], state)
            if b > 0:
                state = (whole[b, 0:1, part] * state.astype(F32) + pull[b, c]).astype(BF16)
    for b in range(blocks):
        cbuf[chan, 0, spans(b), :] = in_acc[b].astype(BF16)
        cbuf[chan, 1, spans(b), :] = out_acc[b].astype(BF16)

    def c_copy(step):
        return remote(cbuf.at[chan], cbuf.at[chan], c_send.at[step], c_recv.at[step], peer(step))

    for step_c in range(1, chan_n):
        c_copy(step_c).start()

    def mixed_grads(g, carry):
        rows = [jnp.zeros((1, GROUP), F32)] * taps
        for b in range(blocks):
            cross = dot(bi_ref[spans(b), :], lead[b, g])
            grad = sgrad[spans(b), lanes(g)] + ee[spans(b), lanes(g)] * cross
            rounded = (gs[spans(b), lanes(g)] * grad).astype(BF16)
            if b == 0:
                mg_out[:, lanes(g)] = rounded[:16]
            wide = rounded.astype(F32)
            mgpad[spans(b), lanes(g)] = wide
            for k in range(taps):
                rows[k] = rows[k] + jnp.sum(wide * shifted(b, k, g), axis=0, keepdims=True)
        for k in range(taps):
            wbuf[mine, pl.ds(k, 1), lanes(g)] = rows[k]
        return carry

    lax.fori_loop(0, groups, mixed_grads, 0)

    def m_copy():
        return remote(mg_out, mg_in, m_sem.at[0], m_sem.at[1], {"seq": seq - 1})

    def w_copy(step):
        return remote(wbuf.at[mine], wbuf.at[mine], w_send.at[step], w_recv.at[step], member(step))

    @pl.when(seq > 0)
    def _():
        m_copy().start()

    def w_start(step, carry):
        w_copy(step).start()
        return carry

    lax.fori_loop(1, team, w_start, 0)

    @pl.when(seq == seq_n - 1)
    def _():
        mgpad[pl.ds(local, 8), :] = jnp.zeros((8, channels), F32)

    @pl.when(seq < seq_n - 1)
    def _():
        m_copy().wait_recv()
        mgpad[pl.ds(local, 8), :] = mg_in[...].astype(F32)[:8]

    def input_grads(g, carry):
        for b in range(blocks):
            total = jnp.zeros((BLOCK, GROUP), F32)
            for k in range(taps):
                total = total + w_ref[k : k + 1, lanes(g)] * mgpad[
                    pl.ds(b * BLOCK + taps - 1 - k, BLOCK), lanes(g)
                ]
            ig_ref[spans(b), lanes(g)] = total.astype(BF16)
        return carry

    lax.fori_loop(0, groups, input_grads, 0)

    for step_c in range(1, chan_n):
        c_copy(step_c).wait_recv()
    for index, ref in enumerate((sig_ref, sog_ref)):
        total = cbuf[0, index].astype(F32)
        for source in range(1, chan_n):
            total = total + cbuf[source, index].astype(F32)
        ref[...] = total

    def w_wait(step, carry):
        w_copy(step).wait_recv()
        return carry

    lax.fori_loop(1, team, w_wait, 0)
    total = lax.fori_loop(
        0, team, lambda i, t: t + wbuf[i], jnp.zeros((taps, channels), F32)
    )
    wg_ref[...] = total * (1.0 / math.sqrt(dp_n * seq_n * local))

    def w_left(step, carry):
        w_copy(step).wait_send()
        return carry

    lax.fori_loop(1, team, w_left, 0)
    for step_c in range(1, chan_n):
        c_copy(step_c).wait_send()

    @pl.when(seq < seq_n - 1)
    def _():
        rim_copy().wait_send()
        for c in range(groups):
            f_copy(c).wait_send()

    @pl.when(seq > 0)
    def _():
        m_copy().wait_send()
        for c in range(groups):
            b_copy(c).wait_send()


def per_device(
    sizes, conv_input, conv_weight, log_decay, state_in, state_out, out_grad, lengths, segment_starts
):
    seq_n, chan_n, dp_n = sizes
    batch, local, channels = conv_input.shape
    heads = log_decay.shape[2]
    states = state_in.shape[2]
    taps = conv_weight.shape[0]
    blocks = local // BLOCK
    groups = channels // GROUP
    team = seq_n * dp_n
    vmem = pl.BlockSpec(memory_space=pltpu.VMEM)
    smem = pl.BlockSpec(memory_space=pltpu.SMEM)
    dma = pltpu.SemaphoreType.DMA
    flat = (local, channels)
    states_shape = (groups, states, GROUP)
    outs = pl.pallas_call(
        functools.partial(kernel, seq_n, chan_n, dp_n),
        out_shape=(
            jax.ShapeDtypeStruct(flat, BF16),
            jax.ShapeDtypeStruct((local, states), F32),
            jax.ShapeDtypeStruct((local, states), F32),
            jax.ShapeDtypeStruct((taps, channels), F32),
        ),
        in_specs=[vmem] * 6 + [smem] * 2,
        out_specs=[vmem] * 4,
        scratch_shapes=[
            pltpu.VMEM((16, channels), BF16),
            pltpu.VMEM((local + 8, channels), F32),
            pltpu.VMEM((local + 8, channels), F32),
            pltpu.VMEM(flat, F32),
            pltpu.VMEM(flat, F32),
            pltpu.VMEM(flat, F32),
            pltpu.VMEM((heads, local, 128), F32),
            pltpu.VMEM((blocks, heads, 1, BLOCK), F32),
            pltpu.VMEM((blocks, BLOCK, BLOCK), F32),
            pltpu.VMEM((blocks, BLOCK, BLOCK), F32),
            pltpu.VMEM((blocks, BLOCK, BLOCK), F32),
            pltpu.VMEM((3, local, 2 * heads), BF16),
            pltpu.VMEM((blocks, 8, channels), F32),
            pltpu.VMEM(flat, BF16),
            pltpu.VMEM(flat, BF16),
            pltpu.VMEM(flat, BF16),
            pltpu.VMEM((blocks,) + states_shape, F32),
            pltpu.VMEM((blocks,) + states_shape, F32),
            pltpu.VMEM((blocks,) + states_shape, BF16),
            pltpu.VMEM(states_shape, BF16),
            pltpu.VMEM(states_shape, BF16),
            pltpu.VMEM(states_shape, BF16),
            pltpu.VMEM(states_shape, BF16),
            pltpu.VMEM((chan_n, 2, local, states), BF16),
            pltpu.VMEM((16, channels), BF16),
            pltpu.VMEM((16, channels), BF16),
            pltpu.VMEM((team, taps, channels), F32),
            dma((2,)),
            dma((2, groups)),
            dma((2, groups)),
            dma((2,)),
            dma((chan_n,)),
            dma((chan_n,)),
            dma((team,)),
            dma((team,)),
        ],
        compiler_params=pltpu.CompilerParams(
            collective_id=0, has_side_effects=True, vmem_limit_bytes=56 * 1024 * 1024
        ),
        cost_estimate=pl.CostEstimate(
            flops=4_000_000_000, bytes_accessed=4_000_000, transcendentals=4_000_000
        ),
    )(
        conv_input[0], conv_weight, log_decay[0], state_in[0], state_out[0], out_grad[0],
        lengths, segment_starts,
    )
    return (outs[0][None], outs[1][None], outs[2][None], outs[3])


def solution(mesh):
    sizes = (mesh.shape["seq"], mesh.shape["chan"], mesh.shape["dp"])
    placed = (
        P(("groups", "dp"), "seq", "chan"),
        P(None, "chan"),
        P(("groups", "dp"), "seq", "chan"),
        P(("groups", "dp"), "seq", None),
        P(("groups", "dp"), "seq", None),
        P(("groups", "dp"), "seq", "chan"),
        P(("groups", "dp")),
        P(("groups", "dp"), None),
    )
    return jax.shard_map(
        functools.partial(per_device, sizes),
        mesh=mesh,
        in_specs=placed,
        out_specs=(
            P(("groups", "dp"), "seq", "chan"),
            P(("groups", "dp"), "seq", None),
            P(("groups", "dp"), "seq", None),
            P("groups", "chan"),
        ),
        check_vma=False,
    )
```

time: 184 us -> 43.7 us (0.24)
  blocking collectives: 53.6 us -> 0 us
  waiting for transfers between devices: 40.5 us -> 0 us
  Pallas kernels: 0 us -> 35.8 us
  other arithmetic: 26.6 us -> 0 us
  matrix products: 21.6 us -> 0 us
  between operations: 18 us -> 1.3 us
  local copies, waits for them, and re-layouts: 15.7 us -> 6.27 us
  starting transfers between devices: 7.02 us -> 0 us
    psum x1 -> x0, blocking collectives: 40 us -> none  [per_device(): weight_grad = lax.psum(jnp.stack(rows) * factor, ('seq', 'dp'))]
    pallas_call x0 -> x1, Pallas kernels: none -> 35.8 us  [per_device(): pl.pallas_call(functools.partial(kernel, seq_n, chan_n, dp_n), out_shape=...]
    dot_general x38 -> x0, matrix products: 21.6 us -> none  [the longest x14 8.56 us: pair_product(): jnp.einsum(form, lower, right, preferred_element_type=jnp.float32)]
    all_gather x2 -> x0, waiting for transfers between devices: 21.5 us -> none  [prefix(): gathered = jax.tree.map(lambda a: lax.all_gather(a, axis), part)]
    psum x1 -> x0, waiting for transfers between devices: 19 us -> none  [per_device(): lax.psum(in_local.astype(jnp.bfloat16), 'chan').astype(jnp.float32)]
    all_gather x1 -> x0, blocking collectives: 13.7 us -> none  [prefix(): gathered = jax.tree.map(lambda a: lax.all_gather(a, axis), part)]
    convert_element_type x4 -> x0, other arithmetic: 7.79 us -> none  [the longest x1 3.89 us: backward_conv(): return summed.astype(jnp.bfloat16)]
    ppermute x2 -> x0, starting transfers between devices: 6.9 us -> none  [shifted(): return lax.ppermute(block, axis, route)]
  transfers between devices with their start and end apart: 5 -> 0, of which waited for: 2 -> 0; matrix products, arithmetic and copies ran while one was open for 21% -> 0% of each run, Pallas kernels for 0% -> 0%
where the time goes in v1:
time: 43.7 us; the launch traced here: 43.4 us
  Pallas kernels  35.8 us (82%)
  local copies, waits for them, and re-layouts  6.27 us (14%)
  between operations  1.3 us (3%)
    pallas_call x1, Pallas kernels, per_device(): pl.pallas_call(functools.partial(kernel, seq_n, chan_n, dp_n), out_shape=...  35.8 us
    unnamed x11, local copies, waits for them, and re-layouts  6.27 us

profile of v1, /device:TPU:0, one launch (start us, length us, event | category | flops | bytes accessed | tf_op | source)
XLA Modules:
  0.0 43.4 jit_solution(4711150377161534255)
XLA Ops:
  1.3 1.6 %copy.12 = f32[1,512,16]{2,1,0:T(8,128)} copy(f32[1,512,16]{1,2,0:T(8,128)} %param.10) | data formatting | bytes 65536 | tf_op args[2]
  2.9 35.8 %shard_map.111 = (bf16[512,1024]{1,0:T(8,128)(2,1)}, f32[512,128]{1,0:T(8,128)}, f32[512,128]{1,0:T(8,128)}, f32[4,1024]{1,0:T(4,128)}) custom-call(bf16[512,1024]{1,0:T(8,128)(2,1)} %bitcast.12, f32[4,1024]{1,0:T(4,128)} %w_ref.1, f32[512,16]{1,0:T(8,128)} %bitcast.9, bf16[512,128]{1,0:T(8,128)(2,1)} %bitcast.14, bf16[512,128]{1,0:T(8,128)(2,1)} %bitcast.15, ...), custom_call_target="tpu_custom_call" | custom-call | flops 4000000000 | bytes 4000000 | tf_op jit(solution)/shard_map/pallas_call | solution.py:440
  38.7 0.0 copy-start.1
  38.7 2.3 %copy.18 = bf16[1,512,1024]{2,1,0:T(8,128)(2,1)} copy(bf16[1,512,1024]{2,1,0:T(8,128)(2,1)} %bitcast.8) | data formatting | bytes 2097152
  41.0 0.0 copy-done.1
  41.0 0.0 copy-start
  41.0 0.7 %copy.19 = f32[1,512,128]{2,1,0:T(8,128)} copy(f32[1,512,128]{2,1,0:T(8,128)S(1)} %bitcast.11) | data formatting | bytes 524288
  41.7 0.3 copy-done
  42.1 0.0 copy-start.2
  42.1 0.7 %copy.20 = f32[1,512,128]{2,1,0:T(8,128)} copy(f32[1,512,128]{2,1,0:T(8,128)S(1)} %bitcast.10) | data formatting | bytes 524288
  42.8 0.0 copy-done.2
  42.8 0.6 %copy.21 = f32[4,1024]{1,0:T(4,128)} copy(f32[4,1024]{1,0:T(4,128)S(1)} %copy-done.2) | data formatting | bytes 32768
Async XLA Ops:
  38.7 2.3 %copy-start.1 = (f32[512,128]{1,0:T(8,128)S(1)}, f32[512,128]{1,0:T(8,128)}, u32[]{:S(2)}) copy-start(f32[512,128]{1,0:T(8,128)} %get-tuple-element.9) | copy-start | bytes 786436
  41.0 1.0 %copy-start = (f32[512,128]{1,0:T(8,128)S(1)}, f32[512,128]{1,0:T(8,128)}, u32[]{:S(2)}) copy-start(f32[512,128]{1,0:T(8,128)} %get-tuple-element.10) | copy-start | bytes 786436
  42.1 0.7 %copy-start.2 = (f32[4,1024]{1,0:T(4,128)S(1)}, f32[4,1024]{1,0:T(4,128)}, u32[]{:S(2)}) copy-start(f32[4,1024]{1,0:T(4,128)} %get-tuple-element.19) | copy-start | bytes 49156

commit v2 on v1

--- a/solution.py
+++ b/solution.py
@@ -43,15 +43,15 @@
 
 def kernel(
     seq_n, chan_n, dp_n,
-    x_ref, w_ref, ld_ref, bi_ref, co_ref, og_ref, len_ref, st_ref,
+    x_hbm, w_ref, ld_ref, bi_ref, co_ref, og_hbm, len_ref, st_ref,
     ig_ref, sig_ref, sog_ref, wg_ref,
-    rim_in, xpad, mgpad, gs, ee, sgrad, colb, rowb, mask, inner, wsum,
+    x_ref, og_ref, load_sem, rim_in, xpad, mgpad, gs, ee, sgrad, colb, rowb, mask, inner, wsum,
     packs, whole, scan, sg, ss, push, pull, lead,
     f_out, f_in, b_out, b_in, cbuf, mg_out, mg_in, wbuf,
     x_sem, f_sem, b_sem, m_sem, c_send, c_recv, w_send, w_recv,
 ):
-    local, channels = x_ref.shape
-    heads = ld_ref.shape[1]
+    local, channels = x_hbm.shape
+    heads = ld_ref.shape[0]
     width = channels // heads
     taps = w_ref.shape[0]
     blocks = local // BLOCK
@@ -72,6 +72,11 @@
     def peer(step):
         return {"chan": lax.rem(chan + step, chan_n)}
 
+    load_x = pltpu.make_async_copy(x_hbm, x_ref, load_sem.at[0])
+    load_og = pltpu.make_async_copy(og_hbm, og_ref, load_sem.at[1])
+    load_og.start()
+    load_x.start()
+
     barrier = pltpu.get_barrier_semaphore()
 
     def greet(step, carry):
@@ -108,7 +113,7 @@
             return total
 
         segment = segments(place)
-        logs = ld_ref[spans(b), :]
+        logs = jnp.transpose(ld_ref[:, spans(b)])
         kept = jnp.where(reset, 0.0, logs)
         order_r = iota((BLOCK, BLOCK), 0)
         order_c = iota((BLOCK, BLOCK), 1)
@@ -150,6 +155,8 @@
 
     pl.semaphore_wait(barrier, team - 1 + chan_n - 1)
 
+    load_og.wait()
+    load_x.wait()
     tail = pl.ds(local - 16, 16)
 
     def rim_copy():
@@ -421,6 +428,15 @@
             b_copy(c).wait_send()
 
 
+def write_out(*refs):
+    sems = refs[-1]
+    copies = [pltpu.make_async_copy(refs[i], refs[i + 4], sems.at[i]) for i in range(4)]
+    for copy in copies:
+        copy.start()
+    for copy in copies:
+        copy.wait()
+
+
 def per_device(
     sizes, conv_input, conv_weight, log_decay, state_in, state_out, out_grad, lengths, segment_starts
 ):
@@ -433,6 +449,7 @@
     groups = channels // GROUP
     team = seq_n * dp_n
     vmem = pl.BlockSpec(memory_space=pltpu.VMEM)
+    hbm = pl.BlockSpec(memory_space=pltpu.HBM)
     smem = pl.BlockSpec(memory_space=pltpu.SMEM)
     dma = pltpu.SemaphoreType.DMA
     flat = (local, channels)
@@ -440,14 +457,17 @@
     outs = pl.pallas_call(
         functools.partial(kernel, seq_n, chan_n, dp_n),
         out_shape=(
-            jax.ShapeDtypeStruct(flat, BF16),
-            jax.ShapeDtypeStruct((local, states), F32),
-            jax.ShapeDtypeStruct((local, states), F32),
-            jax.ShapeDtypeStruct((taps, channels), F32),
+            pltpu.VMEM(flat, BF16),
+            pltpu.VMEM((local, states), F32),
+            pltpu.VMEM((local, states), F32),
+            pltpu.VMEM((taps, channels), F32),
         ),
-        in_specs=[vmem] * 6 + [smem] * 2,
+        in_specs=[hbm] + [vmem] * 4 + [hbm] + [smem] * 2,
         out_specs=[vmem] * 4,
         scratch_shapes=[
+            pltpu.VMEM(flat, BF16),
+            pltpu.VMEM(flat, BF16),
+            dma((2,)),
             pltpu.VMEM((16, channels), BF16),
             pltpu.VMEM((local + 8, channels), F32),
             pltpu.VMEM((local + 8, channels), F32),
@@ -485,15 +505,28 @@
             dma((team,)),
         ],
         compiler_params=pltpu.CompilerParams(
-            collective_id=0, has_side_effects=True, vmem_limit_bytes=56 * 1024 * 1024
+            collective_id=0, has_side_effects=True, vmem_limit_bytes=61 * 1024 * 1024
         ),
         cost_estimate=pl.CostEstimate(
             flops=4_000_000_000, bytes_accessed=4_000_000, transcendentals=4_000_000
         ),
     )(
-        conv_input[0], conv_weight, log_decay[0], state_in[0], state_out[0], out_grad[0],
+        conv_input[0], conv_weight, jnp.transpose(log_decay[0]), state_in[0], state_out[0], out_grad[0],
         lengths, segment_starts,
     )
+    outs = pl.pallas_call(
+        write_out,
+        out_shape=(
+            jax.ShapeDtypeStruct(flat, BF16),
+            jax.ShapeDtypeStruct((local, states), F32),
+            jax.ShapeDtypeStruct((local, states), F32),
+            jax.ShapeDtypeStruct((taps, channels), F32),
+        ),
+        in_specs=[vmem] * 4,
+        out_specs=[hbm] * 4,
+        scratch_shapes=[dma((4,))],
+        compiler_params=pltpu.CompilerParams(vmem_limit_bytes=8 * 1024 * 1024),
+    )(*outs)
     return (outs[0][None], outs[1][None], outs[2][None], outs[3])
 
 

time: 43.7 us -> 36.7 us (0.84)
  local copies, waits for them, and re-layouts: 6.27 us -> 0 us
  Pallas kernels: 35.8 us -> 35.3 us
    unnamed x11 -> x0, local copies, waits for them, and re-layouts: 6.27 us -> none
    pallas_call x1, Pallas kernels: 35.8 us -> 34.1 us  [per_device(): pl.pallas_call(functools.partial(kernel, seq_n, chan_n, dp_n), out_shape=...]
    pallas_call x0 -> x1, Pallas kernels: none -> 1.17 us  [per_device(): pl.pallas_call(write_out, out_shape=(jax.ShapeDtypeStruct(flat, BF16), ja...]
where the time goes in v2:
time: 36.7 us; the launch traced here: 36.6 us
  Pallas kernels  35.3 us (96%)
  between operations  1.29 us (4%)
    pallas_call x1, Pallas kernels, per_device(): pl.pallas_call(functools.partial(kernel, seq_n, chan_n, dp_n), out_shape=...  34.1 us
    pallas_call x1, Pallas kernels, per_device(): pl.pallas_call(write_out, out_shape=(jax.ShapeDtypeStruct(flat, BF16), ja...  1.17 us

profile of v2, /device:TPU:0, one launch (start us, length us, event | category | flops | bytes accessed | tf_op | source)
XLA Modules:
  0.0 36.6 jit_solution(2789112794758468460)
XLA Ops:
  1.3 34.1 %shard_map.111 = (bf16[512,1024]{1,0:T(8,128)(2,1)S(1)}, f32[512,128]{1,0:T(8,128)S(1)}, f32[512,128]{1,0:T(8,128)S(1)}, f32[4,1024]{1,0:T(4,128)S(1)}) custom-call(bf16[512,1024]{1,0:T(8,128)(2,1)} %bitcast.10, f32[4,1024]{1,0:T(4,128)} %w_ref.1, f32[16,512]{1,0:T(8,128)} %bitcast.17, bf16[512,128]{1,0:T(8,128)(2,1)} %bitcast.15, ...), custom_call_target="tpu_custom_call" | custom-call | flops 4000000000 | bytes 4000000 | tf_op jit(solution)/shard_map/pallas_call | solution.py:457
  35.4 1.2 %shard_map.112 = (bf16[512,1024]{1,0:T(8,128)(2,1)}, f32[512,128]{1,0:T(8,128)}, f32[512,128]{1,0:T(8,128)}, f32[4,1024]{1,0:T(4,128)}) custom-call(bf16[512,1024]{1,0:T(8,128)(2,1)S(1)} %get-tuple-element.12.refs_0_, f32[512,128]{1,0:T(8,128)S(1)} %get-tuple-element.13.refs_1_, f32[512,128]{1,0:T(8,128)S(1)} %get-tuple-element.14.refs_2_, ...), custom_call_target="tpu_custom_call" | custom-call | tf_op jit(solution)/shard_map/pallas_call | solution.py:517

commit v3 on v2

--- a/solution.py
+++ b/solution.py
@@ -9,7 +9,7 @@
 from jax.sharding import PartitionSpec as P
 
 BLOCK = 256
-GROUP = 256
+GROUP = 128
 F32 = jnp.float32
 BF16 = jnp.bfloat16
 MESH = pl.DeviceIdType.MESH
@@ -223,7 +223,7 @@
     def shifted(b, k, g):
         return xpad[pl.ds(8 + b * BLOCK - (taps - 1) + k, BLOCK), lanes(g)]
 
-    def pushed(g, carry):
+    def pushed(g):
         e = spread(g)
         for b in range(blocks):
             mixed = w_ref[0:1, lanes(g)] * shifted(b, 0, g)
@@ -245,12 +245,8 @@
             advance(g)
             f_copy(g).start()
 
-        return carry
-
-    lax.fori_loop(0, groups, pushed, 0)
-
-    hop = 2
-    first = 1
+
+    hop = 4
 
     def work(p):
         pair = pl.ds(pl.multiple_of(p * 128, 128), 128)
@@ -274,83 +270,110 @@
             sgrad[spans(b), pair] = total
 
     def step(k, carry):
-        @pl.when(k < pairs)
-        def _():
-            work(k)
-
-        c_f = k - first - hop * (seq - 1)
-
-        @pl.when((seq > 0) & (c_f >= 0) & (c_f < groups))
+        @pl.when(k < groups)
+        def _():
+            pushed(k)
+
+        @pl.when((k >= groups) & (k < groups + pairs))
+        def _():
+            work(k - groups)
+
+        c_f = k - hop * seq
+
+        @pl.when((seq > 0) & (seq < seq_n - 1) & (c_f >= 0) & (c_f < groups))
         def _():
             f_copy(c_f).wait_recv()
-
+            advance(c_f)
+            f_copy(c_f).start()
+
+        c_b = k - hop * (seq_n - 2 - seq)
+
+        @pl.when((seq > 0) & (seq < seq_n - 1) & (c_b >= 0) & (c_b < groups))
+        def _():
+            b_copy(c_b).wait_recv()
+            retreat(c_b)
+            b_copy(c_b).start()
+
+        return carry
+
+    steps = max(groups + pairs, hop * max(seq_n - 2, 0) + groups)
+    lax.fori_loop(0, steps, step, 0)
+
+    def c_copy(index, step):
+        return remote(
+            cbuf.at[chan, index], cbuf.at[chan, index],
+            c_send.at[index, step], c_recv.at[index, step], peer(step),
+        )
+
+    def out_stage():
+        @pl.when(seq == seq_n - 1)
+        def _():
+            @pl.when(seq > 0)
+            def _():
+                for c in range(groups):
+                    f_copy(c).wait_recv()
+
+        acc = []
+        for b in range(blocks):
+            acc.append(dot(jnp.transpose(wsum[b]).astype(BF16), bi_ref[spans(b), :]))
+        for c in range(groups):
+            part = slice(c * GROUP, (c + 1) * GROUP)
+            state = f_in[c]
+            for b in range(blocks):
+                acc[b] = acc[b] + dot_lanes(sg[spans(b), part], state)
+                if b < blocks - 1:
+                    state = (whole[b, 0:1, part] * state.astype(F32) + push[b, c]).astype(BF16)
+        for b in range(blocks):
+            cbuf[chan, 1, spans(b), :] = acc[b].astype(BF16)
+        for step_c in range(1, chan_n):
+            c_copy(1, step_c).start()
+
+    def in_stage():
+        @pl.when(seq == 0)
+        def _():
             @pl.when(seq < seq_n - 1)
             def _():
-                advance(c_f)
-                f_copy(c_f).start()
-
-        c_b = k - hop * (seq_n - 2 - seq)
-
-        @pl.when((seq < seq_n - 1) & (c_b >= 0) & (c_b < groups))
-        def _():
-            b_copy(c_b).wait_recv()
-
-            @pl.when(seq > 0)
-            def _():
-                retreat(c_b)
-                b_copy(c_b).start()
-
-        return carry
-
-    steps = max(pairs, first + hop * max(seq_n - 2, 0) + groups)
-    lax.fori_loop(0, steps, step, 0)
-
-    in_acc = []
-    out_acc = []
-    for b in range(blocks):
-        weights = wsum[b]
-        in_acc.append(dot(weights.astype(BF16), co_ref[spans(b), :]))
-        out_acc.append(dot(jnp.transpose(weights).astype(BF16), bi_ref[spans(b), :]))
-    for c in range(groups):
-        part = slice(c * GROUP, (c + 1) * GROUP)
-        state = f_in[c]
-        for b in range(blocks):
-            out_acc[b] = out_acc[b] + dot_lanes(sg[spans(b), part], state)
-            if b < blocks - 1:
-                state = (whole[b, 0:1, part] * state.astype(F32) + push[b, c]).astype(BF16)
-        state = b_in[c]
-        for b in reversed(range(blocks)):
-            lead[b, c] = state
-            in_acc[b] = in_acc[b] + dot_lanes(ss[spans(b), part], state)
+                for c in range(groups):
+                    b_copy(c).wait_recv()
+
+        acc = []
+        for b in range(blocks):
+            acc.append(dot(wsum[b].astype(BF16), co_ref[spans(b), :]))
+        for c in range(groups):
+            part = slice(c * GROUP, (c + 1) * GROUP)
+            state = b_in[c]
+            for b in reversed(range(blocks)):
+                lead[b, c] = state
+                acc[b] = acc[b] + dot_lanes(ss[spans(b), part], state)
+                if b > 0:
+                    state = (whole[b, 0:1, part] * state.astype(F32) + pull[b, c]).astype(BF16)
+        for b in range(blocks):
+            cbuf[chan, 0, spans(b), :] = acc[b].astype(BF16)
+        for step_c in range(1, chan_n):
+            c_copy(0, step_c).start()
+
+    early = seq < seq_n // 2
+
+    @pl.when(early)
+    def _():
+        out_stage()
+
+    in_stage()
+
+    def mixed_grads(b, g, carry):
+        cross = dot(bi_ref[spans(b), :], lead[b, g])
+        grad = sgrad[spans(b), lanes(g)] + ee[spans(b), lanes(g)] * cross
+        rounded = (gs[spans(b), lanes(g)] * grad).astype(BF16)
+        if b == 0:
+            mg_out[:, lanes(g)] = rounded[:16]
+        wide = rounded.astype(F32)
+        mgpad[spans(b), lanes(g)] = wide
+        for k in range(taps):
+            row = jnp.sum(wide * shifted(b, k, g), axis=0, keepdims=True)
             if b > 0:
-                state = (whole[b, 0:1, part] * state.astype(F32) + pull[b, c]).astype(BF16)
-    for b in range(blocks):
-        cbuf[chan, 0, spans(b), :] = in_acc[b].astype(BF16)
-        cbuf[chan, 1, spans(b), :] = out_acc[b].astype(BF16)
-
-    def c_copy(step):
-        return remote(cbuf.at[chan], cbuf.at[chan], c_send.at[step], c_recv.at[step], peer(step))
-
-    for step_c in range(1, chan_n):
-        c_copy(step_c).start()
-
-    def mixed_grads(g, carry):
-        rows = [jnp.zeros((1, GROUP), F32)] * taps
-        for b in range(blocks):
-            cross = dot(bi_ref[spans(b), :], lead[b, g])
-            grad = sgrad[spans(b), lanes(g)] + ee[spans(b), lanes(g)] * cross
-            rounded = (gs[spans(b), lanes(g)] * grad).astype(BF16)
-            if b == 0:
-                mg_out[:, lanes(g)] = rounded[:16]
-            wide = rounded.astype(F32)
-            mgpad[spans(b), lanes(g)] = wide
-            for k in range(taps):
-                rows[k] = rows[k] + jnp.sum(wide * shifted(b, k, g), axis=0, keepdims=True)
-        for k in range(taps):
-            wbuf[mine, pl.ds(k, 1), lanes(g)] = rows[k]
-        return carry
-
-    lax.fori_loop(0, groups, mixed_grads, 0)
+                row = row + wbuf[mine, pl.ds(k, 1), lanes(g)]
+            wbuf[mine, pl.ds(k, 1), lanes(g)] = row
+        return carry
 
     def m_copy():
         return remote(mg_out, mg_in, m_sem.at[0], m_sem.at[1], {"seq": seq - 1})
@@ -358,9 +381,14 @@
     def w_copy(step):
         return remote(wbuf.at[mine], wbuf.at[mine], w_send.at[step], w_recv.at[step], member(step))
 
+    lax.fori_loop(0, groups, functools.partial(mixed_grads, 0), 0, unroll=2)
+
     @pl.when(seq > 0)
     def _():
         m_copy().start()
+
+    for b in range(1, blocks):
+        lax.fori_loop(0, groups, functools.partial(mixed_grads, b), 0, unroll=2)
 
     def w_start(step, carry):
         w_copy(step).start()
@@ -368,30 +396,35 @@
 
     lax.fori_loop(1, team, w_start, 0)
 
-    @pl.when(seq == seq_n - 1)
-    def _():
-        mgpad[pl.ds(local, 8), :] = jnp.zeros((8, channels), F32)
-
-    @pl.when(seq < seq_n - 1)
-    def _():
-        m_copy().wait_recv()
-        mgpad[pl.ds(local, 8), :] = mg_in[...].astype(F32)[:8]
-
-    def input_grads(g, carry):
-        for b in range(blocks):
-            total = jnp.zeros((BLOCK, GROUP), F32)
-            for k in range(taps):
-                total = total + w_ref[k : k + 1, lanes(g)] * mgpad[
-                    pl.ds(b * BLOCK + taps - 1 - k, BLOCK), lanes(g)
-                ]
-            ig_ref[spans(b), lanes(g)] = total.astype(BF16)
-        return carry
-
-    lax.fori_loop(0, groups, input_grads, 0)
-
-    for step_c in range(1, chan_n):
-        c_copy(step_c).wait_recv()
+    @pl.when(jnp.logical_not(early))
+    def _():
+        out_stage()
+
+    def input_grads(b, g, carry):
+        total = jnp.zeros((BLOCK, GROUP), F32)
+        for k in range(taps):
+            total = total + w_ref[k : k + 1, lanes(g)] * mgpad[
+                pl.ds(b * BLOCK + taps - 1 - k, BLOCK), lanes(g)
+            ]
+        ig_ref[spans(b), lanes(g)] = total.astype(BF16)
+        return carry
+
+    for b in range(blocks):
+        if b == blocks - 1:
+            @pl.when(seq == seq_n - 1)
+            def _():
+                mgpad[pl.ds(local, 8), :] = jnp.zeros((8, channels), F32)
+
+            @pl.when(seq < seq_n - 1)
+            def _():
+                m_copy().wait_recv()
+                mgpad[pl.ds(local, 8), :] = mg_in[...].astype(F32)[:8]
+
+        lax.fori_loop(0, groups, functools.partial(input_grads, b), 0, unroll=2)
+
     for index, ref in enumerate((sig_ref, sog_ref)):
+        for step_c in range(1, chan_n):
+            c_copy(index, step_c).wait_recv()
         total = cbuf[0, index].astype(F32)
         for source in range(1, chan_n):
             total = total + cbuf[source, index].astype(F32)
@@ -412,8 +445,9 @@
         return carry
 
     lax.fori_loop(1, team, w_left, 0)
-    for step_c in range(1, chan_n):
-        c_copy(step_c).wait_send()
+    for index in range(2):
+        for step_c in range(1, chan_n):
+            c_copy(index, step_c).wait_send()
 
     @pl.when(seq < seq_n - 1)
     def _():
@@ -499,8 +533,8 @@
             dma((2, groups)),
             dma((2, groups)),
             dma((2,)),
-            dma((chan_n,)),
-            dma((chan_n,)),
+            dma((2, chan_n)),
+            dma((2, chan_n)),
             dma((team,)),
             dma((team,)),
         ],

time: 36.7 us -> 33.1 us (0.902)
  Pallas kernels: 35.3 us -> 31.7 us
    pallas_call x1, Pallas kernels: 34.1 us -> 30.5 us  [per_device(): pl.pallas_call(functools.partial(kernel, seq_n, chan_n, dp_n), out_shape=...]
where the time goes in v3:
time: 33.1 us; the launch traced here: 33 us
  Pallas kernels  31.7 us (96%)
  between operations  1.29 us (4%)
    pallas_call x1, Pallas kernels, per_device(): pl.pallas_call(functools.partial(kernel, seq_n, chan_n, dp_n), out_shape=...  30.5 us
    pallas_call x1, Pallas kernels, per_device(): pl.pallas_call(write_out, out_shape=(jax.ShapeDtypeStruct(flat, BF16), ja...  1.17 us

profile of v3, /device:TPU:0, one launch (start us, length us, event | category | flops | bytes accessed | tf_op | source)
XLA Modules:
  0.0 33.0 jit_solution(1961541138493422253)
XLA Ops:
  1.3 30.5 %shard_map.111 = (bf16[512,1024]{1,0:T(8,128)(2,1)S(1)}, f32[512,128]{1,0:T(8,128)S(1)}, f32[512,128]{1,0:T(8,128)S(1)}, f32[4,1024]{1,0:T(4,128)S(1)}) custom-call(bf16[512,1024]{1,0:T(8,128)(2,1)} %bitcast.10, f32[4,1024]{1,0:T(4,128)} %w_ref.1, f32[16,512]{1,0:T(8,128)} %bitcast.17, bf16[512,128]{1,0:T(8,128)(2,1)} %bitcast.15, ...), custom_call_target="tpu_custom_call" | custom-call | flops 4000000000 | bytes 4000000 | tf_op jit(solution)/shard_map/pallas_call | solution.py:491
  31.8 1.2 %shard_map.112 = (bf16[512,1024]{1,0:T(8,128)(2,1)}, f32[512,128]{1,0:T(8,128)}, f32[512,128]{1,0:T(8,128)}, f32[4,1024]{1,0:T(4,128)}) custom-call(bf16[512,1024]{1,0:T(8,128)(2,1)S(1)} %get-tuple-element.12.refs_0_, f32[512,128]{1,0:T(8,128)S(1)} %get-tuple-element.13.refs_1_, f32[512,128]{1,0:T(8,128)S(1)} %get-tuple-element.14.refs_2_, ...), custom_call_target="tpu_custom_call" | custom-call | tf_op jit(solution)/shard_map/pallas_call | solution.py:551

commit v4 on v3

--- a/solution.py
+++ b/solution.py
@@ -9,7 +9,7 @@
 from jax.sharding import PartitionSpec as P
 
 BLOCK = 256
-GROUP = 128
+GROUP = 256
 F32 = jnp.float32
 BF16 = jnp.bfloat16
 MESH = pl.DeviceIdType.MESH
@@ -381,14 +381,14 @@
     def w_copy(step):
         return remote(wbuf.at[mine], wbuf.at[mine], w_send.at[step], w_recv.at[step], member(step))
 
-    lax.fori_loop(0, groups, functools.partial(mixed_grads, 0), 0, unroll=2)
+    lax.fori_loop(0, groups, functools.partial(mixed_grads, 0), 0, unroll=4)
 
     @pl.when(seq > 0)
     def _():
         m_copy().start()
 
     for b in range(1, blocks):
-        lax.fori_loop(0, groups, functools.partial(mixed_grads, b), 0, unroll=2)
+        lax.fori_loop(0, groups, functools.partial(mixed_grads, b), 0, unroll=4)
 
     def w_start(step, carry):
         w_copy(step).start()
@@ -420,7 +420,7 @@
                 m_copy().wait_recv()
                 mgpad[pl.ds(local, 8), :] = mg_in[...].astype(F32)[:8]
 
-        lax.fori_loop(0, groups, functools.partial(input_grads, b), 0, unroll=2)
+        lax.fori_loop(0, groups, functools.partial(input_grads, b), 0, unroll=4)
 
     for index, ref in enumerate((sig_ref, sog_ref)):
         for step_c in range(1, chan_n):

time: 33.1 us -> 30.6 us (0.924)
  Pallas kernels: 31.7 us -> 29.1 us
    pallas_call x1, Pallas kernels: 30.5 us -> 27.9 us  [per_device(): pl.pallas_call(functools.partial(kernel, seq_n, chan_n, dp_n), out_shape=...]
where the time goes in v4:
time: 30.6 us; the launch traced here: 30.4 us
  Pallas kernels  29.1 us (95%)
  between operations  1.29 us (4%)
    pallas_call x1, Pallas kernels, per_device(): pl.pallas_call(functools.partial(kernel, seq_n, chan_n, dp_n), out_shape=...  27.9 us
    pallas_call x1, Pallas kernels, per_device(): pl.pallas_call(write_out, out_shape=(jax.ShapeDtypeStruct(flat, BF16), ja...  1.17 us

profile of v4, /device:TPU:0, one launch (start us, length us, event | category | flops | bytes accessed | tf_op | source)
XLA Modules:
  0.0 30.4 jit_solution(11591501134744315323)
XLA Ops:
  1.3 27.9 %shard_map.111 = (bf16[512,1024]{1,0:T(8,128)(2,1)S(1)}, f32[512,128]{1,0:T(8,128)S(1)}, f32[512,128]{1,0:T(8,128)S(1)}, f32[4,1024]{1,0:T(4,128)S(1)}) custom-call(bf16[512,1024]{1,0:T(8,128)(2,1)} %bitcast.10, f32[4,1024]{1,0:T(4,128)} %w_ref.1, f32[16,512]{1,0:T(8,128)} %bitcast.17, bf16[512,128]{1,0:T(8,128)(2,1)} %bitcast.15, ...), custom_call_target="tpu_custom_call" | custom-call | flops 4000000000 | bytes 4000000 | tf_op jit(solution)/shard_map/pallas_call | solution.py:491
  29.2 1.2 %shard_map.112 = (bf16[512,1024]{1,0:T(8,128)(2,1)}, f32[512,128]{1,0:T(8,128)}, f32[512,128]{1,0:T(8,128)}, f32[4,1024]{1,0:T(4,128)}) custom-call(bf16[512,1024]{1,0:T(8,128)(2,1)S(1)} %get-tuple-element.12.refs_0_, f32[512,128]{1,0:T(8,128)S(1)} %get-tuple-element.13.refs_1_, f32[512,128]{1,0:T(8,128)S(1)} %get-tuple-element.14.refs_2_, ...), custom_call_target="tpu_custom_call" | custom-call | tf_op jit(solution)/shard_map/pallas_call | solution.py:551

commit v5 on v4

--- a/solution.py
+++ b/solution.py
@@ -246,7 +246,7 @@
             f_copy(g).start()
 
 
-    hop = 4
+    hop = 5
 
     def work(p):
         pair = pl.ds(pl.multiple_of(p * 128, 128), 128)

time: 30.6 us -> 31.6 us (1.033)
  the two profiles are of different devices: /device:TPU:0 before, /device:TPU:24 now
where the time goes in v5:
time: 31.6 us; the launch traced here: 31.4 us
  Pallas kernels  30.1 us (95%)
  between operations  1.29 us (4%)
    pallas_call x1, Pallas kernels, per_device(): pl.pallas_call(functools.partial(kernel, seq_n, chan_n, dp_n), out_shape=...  29 us
    pallas_call x1, Pallas kernels, per_device(): pl.pallas_call(write_out, out_shape=(jax.ShapeDtypeStruct(flat, BF16), ja...  1.17 us

profile of v5, /device:TPU:24, one launch (start us, length us, event | category | flops | bytes accessed | tf_op | source)
XLA Modules:
  0.0 31.4 jit_solution(7237246657287145505)
XLA Ops:
  1.3 29.0 %shard_map.111 = (bf16[512,1024]{1,0:T(8,128)(2,1)S(1)}, f32[512,128]{1,0:T(8,128)S(1)}, f32[512,128]{1,0:T(8,128)S(1)}, f32[4,1024]{1,0:T(4,128)S(1)}) custom-call(bf16[512,1024]{1,0:T(8,128)(2,1)} %bitcast.10, f32[4,1024]{1,0:T(4,128)} %w_ref.1, f32[16,512]{1,0:T(8,128)} %bitcast.17, bf16[512,128]{1,0:T(8,128)(2,1)} %bitcast.15, ...), custom_call_target="tpu_custom_call" | custom-call | flops 4000000000 | bytes 4000000 | tf_op jit(solution)/shard_map/pallas_call | solution.py:491
  30.3 1.2 %shard_map.112 = (bf16[512,1024]{1,0:T(8,128)(2,1)}, f32[512,128]{1,0:T(8,128)}, f32[512,128]{1,0:T(8,128)}, f32[4,1024]{1,0:T(4,128)}) custom-call(bf16[512,1024]{1,0:T(8,128)(2,1)S(1)} %get-tuple-element.12.refs_0_, f32[512,128]{1,0:T(8,128)S(1)} %get-tuple-element.13.refs_1_, f32[512,128]{1,0:T(8,128)S(1)} %get-tuple-element.14.refs_2_, ...), custom_call_target="tpu_custom_call" | custom-call | tf_op jit(solution)/shard_map/pallas_call | solution.py:551
